TPU v7x, 128 devices: a whole 4x4x4 slice. The times are simulated.
128 devices in a mesh: tm: 64 (over z, y, x), row: 2 (over core).
Axes of the slice: x: 4, y: 4, z: 4, core: 2. Of those that a mesh axis runs over, the one named last changes fastest.
Arguments:
- initial: float32 [1024], replicated, may hold values from -6 to 6
- dynamics: float32 [1024, 1024], replicated, may hold values from -0.009765625 to 0.009765625
- obs_rows: bfloat16 [131072, 1024], P('tm', 'row'), may hold values from -0.1875 to 0.1875
- obs_values: bfloat16 [131072], P('tm'), may hold values from -6 to 6
- obs_slab: int32 [131072, 1], P('tm'), may hold values from 0 to 127; in each aligned block of 2048 rows (0 to 2047, 2048 to 4095, ...) at most 64 rows name the same one
Outputs:
- states: float32 [128, 1024], P('tm', 'row')
Inputs may be any that keep to these rules, and one draw needn't show every extreme that they name: `obs_slab`: within the rows ingested by one index of tm, no slab is named by more than 64 rows, a bound that some block reaches of them.
All inputs are finite; a program needn't handle non-finite values.
Results may differ from a plain program's by a relative error of at most 0.0003.
Values may be sent and summed in bfloat16 or wider, within the bound.
No kernel may reach another device: no remote copies, remote signals or barrier semaphores. Data moves between devices by JAX's collectives and lax.ppermute only.
A program may use at most 128 MiB of HBM per device.

v0:
```python
import jax
import jax.numpy as jnp
from jax import lax
from jax.sharding import PartitionSpec as P

SLAB_DEV = 2
CAP = 64


sigma_gain = 0.3


def shifted(value, axis, steps):
    count = lax.axis_size(axis)
    first, last = (max(0, -steps), min(count, count - steps))
    return lax.ppermute(value, axis, [(source, source + steps) for source in range(first, last)])


def left_product(left_rows, pieces):
    new_matrix = jnp.dot(left_rows, pieces[0], precision=lax.Precision.HIGHEST)
    new_vector = jnp.dot(left_rows, pieces[1], precision=lax.Precision.HIGHEST)
    return (new_matrix, new_vector)


def body(initial, dynamics, obs_rows, obs_values, obs_slab):
    time_devs = lax.axis_size("tm")
    row_devs = lax.axis_size("row")
    state_width = dynamics.shape[1]
    local_cols = state_width // row_devs
    row_start = lax.axis_index("row") * local_cols
    time_index = lax.axis_index("tm")
    capacity = CAP
    slab_total = SLAB_DEV * time_devs
    obs_count = obs_rows.shape[0]
    target = obs_slab[:, 0]
    onehot = (target[:, None] == jnp.arange(slab_total, dtype=jnp.int32)[None, :]).astype(jnp.int32)
    rank_in = jnp.sum(onehot * (jnp.cumsum(onehot, axis=0) - 1), axis=1)
    owner_dev = target // SLAB_DEV
    within = target % SLAB_DEV
    slot_index = (within * time_devs + owner_dev) * capacity + rank_in
    slot_table = (
        jnp.full((slab_total * capacity,), obs_count, jnp.int32)
        .at[slot_index]
        .set(jnp.arange(obs_count, dtype=jnp.int32))
    )
    padded_rows = jnp.concatenate([obs_rows, jnp.zeros((1, local_cols), jnp.bfloat16)], axis=0)
    padded_values = jnp.concatenate([obs_values, jnp.zeros((1,), jnp.bfloat16)], axis=0)
    send_rows = padded_rows[slot_table].reshape(SLAB_DEV, time_devs, capacity, local_cols)
    send_values = padded_values[slot_table].reshape(SLAB_DEV, time_devs, capacity)
    recv_rows, recv_values = (
        lax.all_to_all(send_rows, "tm", split_axis=1, concat_axis=1, tiled=True),
        lax.all_to_all(send_values, "tm", split_axis=1, concat_axis=1, tiled=True),
    )
    slab_rows = recv_rows.reshape(SLAB_DEV, time_devs * capacity, local_cols)
    slab_values = recv_values.reshape(SLAB_DEV, time_devs * capacity)
    information = jnp.einsum(
        "sra,srb->sab",
        slab_rows,
        lax.all_gather(slab_rows, "row", axis=2, tiled=True),
        preferred_element_type=jnp.float32,
    )
    moment = jnp.einsum("sr,sra->sa", slab_values, slab_rows, preferred_element_type=jnp.float32)
    evolve = jnp.eye(state_width, dtype=jnp.float32) + dynamics
    evolve_rows = lax.dynamic_slice_in_dim(evolve, row_start, local_cols, 0)
    transitions = []
    offsets = []
    for slab_index in range(SLAB_DEV):
        transitions.append(
            evolve_rows
            - sigma_gain * jnp.dot(information[slab_index], evolve, precision=lax.Precision.HIGHEST)
        )
        offsets.append(sigma_gain * moment[slab_index])
    composed = transitions[0]
    composed_offset = offsets[0]
    slab_index = 1
    new_matrix, new_vector = left_product(
        transitions[slab_index],
        (
            lax.all_gather(composed, "row", axis=0, tiled=True),
            lax.all_gather(composed_offset, "row", axis=0, tiled=True),
        ),
    )
    composed = new_matrix
    composed_offset = new_vector + offsets[slab_index]
    initial_rows = lax.dynamic_slice_in_dim(initial, row_start, local_cols, 0)
    below_matrix, below_vector = shifted((composed, composed_offset), "tm", 1)
    first_dev = time_index == 0
    prefix_matrix = jnp.where(first_dev, jnp.zeros_like(below_matrix), below_matrix)
    prefix_vector = jnp.where(first_dev, initial_rows, below_vector)
    levels = time_devs.bit_length() - 1
    for level_index in range(levels):
        distance = 1 << level_index
        recv_matrix, recv_vector = shifted((prefix_matrix, prefix_vector), "tm", distance)
        new_matrix, new_vector = left_product(
            prefix_matrix,
            (
                lax.all_gather(recv_matrix, "row", axis=0, tiled=True),
                lax.all_gather(recv_vector, "row", axis=0, tiled=True),
            ),
        )
        active = time_index >= distance
        prefix_matrix = jnp.where(active, new_matrix, prefix_matrix)
        prefix_vector = jnp.where(active, new_vector + prefix_vector, prefix_vector)
    states = []
    current = prefix_vector
    for slab_index in range(SLAB_DEV):
        whole_state = lax.all_gather(current, "row", axis=0, tiled=True)
        current = (
            jnp.dot(transitions[slab_index], whole_state, precision=lax.Precision.HIGHEST)
            + offsets[slab_index]
        )
        states.append(current)
    return jnp.stack(states)


def solution(mesh):
    placed = (P(), P(), P("tm", "row"), P("tm"), P("tm", None))
    return jax.shard_map(
        body, mesh=mesh, in_specs=placed, out_specs=P("tm", "row"), check_vma=False
    )
```

profile of v0, /device:TPU:0, one launch (start us, length us, event | category | flops | bytes accessed | tf_op | source)
XLA Modules:
  0.0 863.2 jit_solution(13235669591487303627)
XLA Ops:
  9.2 8.1 scatter_custom_fusion
  17.3 1.7 concatenate.6
  19.0 33.8 %gather_fusion = bf16[8192,512]{1,0:T(8,128)(2,1)} fusion(bf16[2049,512]{1,0:T(8,128)(2,1)S(1)} %concatenate.6, s32[8192]{0:T(1024)S(1)} %fusion.9), kind=kCustom, calls=%fused_computation | custom fusion | bytes 16809984 | tf_op jit(solution)/shard_map/gather | solution.py:48
  52.8 7.8 copy.18
  60.6 110.1 %all_to_all.10 = bf16[2,64,64,512]{3,2,0,1:T(8,128)(2,1)} all-to-all(bf16[2,64,64,512]{3,2,0,1:T(8,128)(2,1)} %copy.18), channel_id=1, replica_groups=mesh['tm'=64,'row'=2] {'tm'}, dimensions={1} | all-to-all | bytes 16777216 | tf_op jit(solution)/shard_map/all_to_all | solution.py:51
  170.7 7.8 copy.19
  178.8 4.9 convert_add_fusion
  183.7 24.8 %all-gather.17.cloned.1.call-done = bf16[2,4096,1024]{2,1,0:T(8,128)(2,1)} async-done(((bf16[2,4096,512]{2,1,0:T(8,128)(2,1)}), bf16[2,4096,1024]{2,1,0:T(8,128)(2,1)}) %all-gather.17.cloned.1.call-update) | async-done | bytes 16777232 | tf_op jit(solution)/shard_map/all_gather | solution.py:59
  208.5 16.2 %fusion.16 = f32[2,512,1024]{2,1,0:T(8,128)} fusion(bf16[2,4096,512]{2,1,0:T(8,128)(2,1)} %bitcast.111, bf16[2,4096,1024]{2,1,0:T(8,128)(2,1)} %all-gather.17.cloned.1.call-done), kind=kOutput, calls=%fused_computation.54 | convolution fusion | flops 8589934592 | bytes 29360128 | tf_op jit(solution)/shard_map/sra,srb->sab/dot_general | solution.py:56
  224.7 10.6 %multiply_subtract_fusion.1 = f32[512,1024]{1,0:T(8,128)} fusion(f32[1024,1024]{1,0:T(8,128)} %convert_add_fusion, s32[]{:T(128)S(6)} %select_n.108, f32[2,512,1024]{2,1,0:T(8,128)} %fusion.16), kind=kOutput, calls=%fused_computation.12 | convolution fusion | flops 6443499520 | bytes 10485764 | tf_op jit(solution)/shard_map/dot_general | solution.py:70
  235.9 10.1 %multiply_subtract_fusion = f32[512,1024]{1,0:T(8,128)S(1)} fusion(f32[1024,1024]{1,0:T(8,128)} %convert_add_fusion, s32[]{:T(128)S(6)} %select_n.108, f32[2,512,1024]{2,1,0:T(8,128)} %fusion.16), kind=kOutput, calls=%fused_computation.11 | convolution fusion | flops 6443499520 | bytes 10485764 | tf_op jit(solution)/shard_map/dot_general | solution.py:70
  246.1 7.2 all-gather.19.cloned.1.call-done
  253.2 9.6 %fusion.17 = f32[512,1024]{1,0:T(8,128)} fusion(f32[512,1024]{1,0:T(8,128)S(1)} %multiply_subtract_fusion, f32[1024,1024]{1,0:T(8,128)} %all-gather.19.cloned.1.call-done), kind=kOutput, calls=%fused_computation.55 | convolution fusion | flops 6442450944 | bytes 8388608 | tf_op jit(solution)/shard_map/dot_general | solution.py:20
  262.8 4.8 collective-permute-start
  267.7 44.3 %collective-permute-done = f32[512,1024]{1,0:T(8,128)} collective-permute-done((f32[512,1024]{1,0:T(8,128)}, f32[512,1024]{1,0:T(8,128)}, u32[]{:S(2)}, u32[]{:S(2)}) %collective-permute-start) | collective-permute-done | bytes 2097184 | tf_op jit(solution)/shard_map/ppermute | solution.py:16
  312.1 7.4 collective-permute-start.1
  319.5 43.1 %collective-permute-done.1 = f32[512,1024]{1,0:T(8,128)} collective-permute-done((f32[512,1024]{1,0:T(8,128)S(1)}, f32[512,1024]{1,0:T(8,128)}, u32[]{:S(2)}, u32[]{:S(2)}) %collective-permute-start.1) | collective-permute-done | bytes 2097184 | tf_op jit(solution)/shard_map/ppermute | solution.py:16
  362.7 22.4 %all-gather.21.cloned.1.call-done = f32[1024,1024]{1,0:T(8,128)} async-done(((f32[512,1024]{1,0:T(8,128)}), f32[1024,1024]{1,0:T(8,128)}) %all-gather.21.cloned.1.call-update) | async-done | bytes 4194320 | tf_op jit(solution)/shard_map/all_gather | solution.py:97
  385.1 9.1 %convolution_select_fusion.3 = f32[512,1024]{1,0:T(8,128)S(1)} fusion(f32[512,1024]{1,0:T(8,128)S(1)} %broadcast_select_fusion, f32[1024,1024]{1,0:T(8,128)} %all-gather.21.cloned.1.call-done, pred[]{:T(512)S(6)} %ge.23), kind=kOutput, calls=%fused_computation.16 | convolution fusion | flops 6442975232 | bytes 8388609 | tf_op jit(solution)/shard_map/dot_general | solution.py:20
  394.3 6.3 collective-permute-start.2
  400.6 44.0 %collective-permute-done.2 = f32[512,1024]{1,0:T(8,128)} collective-permute-done((f32[512,1024]{1,0:T(8,128)S(1)}, f32[512,1024]{1,0:T(8,128)}, u32[]{:S(2)}, u32[]{:S(2)}) %collective-permute-start.2) | collective-permute-done | bytes 2097184 | tf_op jit(solution)/shard_map/ppermute | solution.py:16
  444.9 18.6 %all-gather.23.cloned.1.call-done = f32[1024,1024]{1,0:T(8,128)} async-done(((f32[512,1024]{1,0:T(8,128)}), f32[1024,1024]{1,0:T(8,128)}) %all-gather.23.cloned.1.call-update) | async-done | bytes 4194320 | tf_op jit(solution)/shard_map/all_gather | solution.py:97
  463.5 9.1 %convolution_select_fusion.2 = f32[512,1024]{1,0:T(8,128)S(1)} fusion(f32[512,1024]{1,0:T(8,128)S(1)} %copy-done.7, f32[1024,1024]{1,0:T(8,128)} %all-gather.23.cloned.1.call-done, pred[]{:T(512)S(6)} %ge.22), kind=kOutput, calls=%fused_computation.15 | convolution fusion | flops 6442975232 | bytes 8388609 | tf_op jit(solution)/shard_map/dot_general | solution.py:20
  472.7 1.3 copy-done.9
  474.0 4.8 collective-permute-start.3
  478.8 44.0 %collective-permute-done.3 = f32[512,1024]{1,0:T(8,128)} collective-permute-done((f32[512,1024]{1,0:T(8,128)S(1)}, f32[512,1024]{1,0:T(8,128)}, u32[]{:S(2)}, u32[]{:S(2)}) %collective-permute-start.3) | collective-permute-done | bytes 2097184 | tf_op jit(solution)/shard_map/ppermute | solution.py:16
  522.9 18.8 %all-gather.25.cloned.1.call-done = f32[1024,1024]{1,0:T(8,128)} async-done(((f32[512,1024]{1,0:T(8,128)}), f32[1024,1024]{1,0:T(8,128)}) %all-gather.25.cloned.1.call-update) | async-done | bytes 4194320 | tf_op jit(solution)/shard_map/all_gather | solution.py:97
  541.7 9.1 %convolution_select_fusion.1 = f32[512,1024]{1,0:T(8,128)S(1)} fusion(f32[512,1024]{1,0:T(8,128)S(1)} %copy-done.10, f32[1024,1024]{1,0:T(8,128)} %all-gather.25.cloned.1.call-done, pred[]{:T(512)S(6)} %ge.21), kind=kOutput, calls=%fused_computation.14 | convolution fusion | flops 6442975232 | bytes 8388609 | tf_op jit(solution)/shard_map/dot_general | solution.py:20
  552.1 5.1 collective-permute-start.4
  557.3 45.2 %collective-permute-done.4 = f32[512,1024]{1,0:T(8,128)S(1)} collective-permute-done((f32[512,1024]{1,0:T(8,128)S(1)}, f32[512,1024]{1,0:T(8,128)S(1)}, u32[]{:S(2)}, u32[]{:S(2)}) %collective-permute-start.4) | collective-permute-done | bytes 2097184 | tf_op jit(solution)/shard_map/ppermute | solution.py:16
  602.5 1.4 copy-done.14
  603.9 18.7 %all-gather.27.cloned.1.call-done = f32[1024,1024]{1,0:T(8,128)} async-done(((f32[512,1024]{1,0:T(8,128)}), f32[1024,1024]{1,0:T(8,128)}) %all-gather.27.cloned.1.call-update) | async-done | bytes 4194320 | tf_op jit(solution)/shard_map/all_gather | solution.py:97
  622.6 10.1 %convolution_select_fusion = f32[512,1024]{1,0:T(8,128)S(1)} fusion(f32[512,1024]{1,0:T(8,128)} %copy-done.12, f32[1024,1024]{1,0:T(8,128)} %all-gather.27.cloned.1.call-done, pred[]{:T(512)S(6)} %ge.20), kind=kOutput, calls=%fused_computation.13 | convolution fusion | flops 6442975232 | bytes 8388609 | tf_op jit(solution)/shard_map/dot_general | solution.py:20
  632.7 4.9 collective-permute-start.5
  637.6 44.0 %collective-permute-done.5 = f32[512,1024]{1,0:T(8,128)} collective-permute-done((f32[512,1024]{1,0:T(8,128)S(1)}, f32[512,1024]{1,0:T(8,128)}, u32[]{:S(2)}, u32[]{:S(2)}) %collective-permute-start.5) | collective-permute-done | bytes 2097184 | tf_op jit(solution)/shard_map/ppermute | solution.py:16
  681.6 50.7 %gather_fusion.1 = bf16[8192]{0:T(1024)(128)(2,1)S(1)} fusion(bf16[2049]{0:T(1024)(128)(2,1)S(1)} %pad_maximum_fusion, s32[8192]{0:T(1024)S(1)} %fusion.9), kind=kCustom, calls=%fused_computation.1 | custom fusion | bytes 65536 | tf_op jit(solution)/shard_map/gather | solution.py:49
  732.5 20.7 %all_to_all.11 = bf16[2,64,64]{2,0,1:T(2,128)(2,1)S(1)} all-to-all(bf16[2,64,64]{2,0,1:T(2,128)(2,1)S(1)} %copy.21), channel_id=1, replica_groups=mesh['tm'=64,'row'=2] {'tm'}, dimensions={1} | all-to-all | bytes 32768 | tf_op jit(solution)/shard_map/all_to_all | solution.py:52
  753.3 4.7 fusion.19
  758.0 1.9 all-gather
  760.0 1.9 fusion.14
  761.8 2.5 collective-permute-start.6
  765.7 4.2 collective-permute-start.7
  771.2 1.8 all-gather.1
  772.9 1.9 fusion.20
  774.8 4.7 collective-permute-start.8
  780.8 1.8 all-gather.2
  782.6 1.9 fusion.21
  784.5 10.3 %collective-permute-start.9 = (f32[512]{0:T(512)S(1)}, f32[512]{0:T(512)S(1)}, u32[]{:S(2)}, u32[]{:S(2)}) collective-permute-start(f32[512]{0:T(512)S(1)} %add_select_fusion.4), channel_id=1, source_target_pairs={{0,8},{2,10},{4,12},{6,14},{8,16},{10,18},{12,20},{14,22},{16,24},... | collective-permute-start | bytes 6152 | tf_op jit(solution)/shard_map/ppermute | solution.py:16
  796.1 1.8 all-gather.3
  797.8 1.9 fusion.22
  799.7 4.8 collective-permute-start.10
  805.8 1.8 all-gather.4
  807.6 1.9 fusion.23
  809.4 14.4 %collective-permute-start.11 = (f32[512]{0:T(512)S(1)}, f32[512]{0:T(512)S(1)}, u32[]{:S(2)}, u32[]{:S(2)}) collective-permute-start(f32[512]{0:T(512)S(1)} %add_select_fusion.2), channel_id=1, source_target_pairs={{0,32},{2,34},{4,36},{6,38},{8,40},{10,42},{12,44},{14,46},{16,48}... | collective-permute-start | bytes 6152 | tf_op jit(solution)/shard_map/ppermute | solution.py:16
  825.2 1.8 all-gather.5
  826.9 1.9 fusion.24
  828.8 4.8 collective-permute-start.12
  834.9 2.0 all-gather.6
  837.0 9.1 %fusion.18 = f32[512,1024]{1,0:T(8,128)S(1)} fusion(f32[512,1024]{1,0:T(8,128)S(1)} %convolution_select_fusion, f32[1024,1024]{1,0:T(8,128)} %all-gather.29.cloned.1.call-done), kind=kOutput, calls=%fused_computation.56 | convolution fusion | flops 6442450944 | bytes 8388608 | tf_op jit(solution)/shard_map/dot_general | solution.py:20
  846.1 1.9 fusion.2
  848.0 1.9 all-gather.7
  849.9 1.9 fusion.25
  851.8 1.8 all-gather.8
  853.6 1.9 fusion.26
  (86 shorter events, 15.5 us)
Async XLA Ops:
  6.5 202.0 %all-gather.17.cloned.1.call-start = ((), (), s32[]{:S(2)}) async-start(), calls=%async_computation.2 | async-start | bytes 25165824 | tf_op jit(solution)/shard_map/all_gather | solution.py:59
  7.7 0.7 copy-start.15
  178.5 74.7 %all-gather.19.cloned.1.call-start = ((), (), s32[]{:S(2)}) async-start(), calls=%async_computation.3 | async-start | bytes 6291456 | tf_op jit(solution)/shard_map/all_gather | solution.py:79
  235.4 149.8 %all-gather.21.cloned.1.call-start = ((), (), s32[]{:S(2)}) async-start(), calls=%async_computation.4 | async-start | bytes 6291456 | tf_op jit(solution)/shard_map/all_gather | solution.py:97
  246.1 16.8 %copy-start = (f32[512,1024]{1,0:T(8,128)}, f32[512,1024]{1,0:T(8,128)S(1)}, u32[]{:S(2)}) copy-start(f32[512,1024]{1,0:T(8,128)S(1)} %multiply_subtract_fusion) | copy-start | bytes 6291460
  262.8 49.1 %collective-permute-start = (f32[512,1024]{1,0:T(8,128)}, f32[512,1024]{1,0:T(8,128)}, u32[]{:S(2)}, u32[]{:S(2)}) collective-permute-start(f32[512,1024]{1,0:T(8,128)} %fusion.17), channel_id=1, source_target_pairs={{0,2},{2,4},{4,6},{6,8},{8,10},{10,12},{12,14},{14,16},{16,18},{18... | collective-permute-start | bytes 6291464 | tf_op jit(solution)/shard_map/ppermute | solution.py:16
  312.1 82.1 %copy-start.4 = (f32[512,1024]{1,0:T(8,128)}, f32[512,1024]{1,0:T(8,128)S(1)}, u32[]{:S(2)}) copy-start(f32[512,1024]{1,0:T(8,128)S(1)} %broadcast_select_fusion) | copy-start | bytes 6291460
  312.1 50.5 %collective-permute-start.1 = (f32[512,1024]{1,0:T(8,128)S(1)}, f32[512,1024]{1,0:T(8,128)}, u32[]{:S(2)}, u32[]{:S(2)}) collective-permute-start(f32[512,1024]{1,0:T(8,128)S(1)} %broadcast_select_fusion), channel_id=1, source_target_pairs={{0,2},{2,4},{4,6},{6,8},{8,10},{10,12},{12,14},{14,16},{16,18},{18... | collective-permute-start | bytes 6291464 | tf_op jit(solution)/shard_map/ppermute | solution.py:16
  362.7 100.8 %all-gather.23.cloned.1.call-start = ((), (), s32[]{:S(2)}) async-start(), calls=%async_computation.5 | async-start | bytes 6291456 | tf_op jit(solution)/shard_map/all_gather | solution.py:97
  394.3 6.3 copy-start.6
  394.3 50.3 %collective-permute-start.2 = (f32[512,1024]{1,0:T(8,128)S(1)}, f32[512,1024]{1,0:T(8,128)}, u32[]{:S(2)}, u32[]{:S(2)}) collective-permute-start(f32[512,1024]{1,0:T(8,128)S(1)} %convolution_select_fusion.3), channel_id=1, source_target_pairs={{0,4},{2,6},{4,8},{6,10},{8,12},{10,14},{12,16},{14,18},{16,20},{1... | collective-permute-start | bytes 6291464 | tf_op jit(solution)/shard_map/ppermute | solution.py:16
  444.6 18.9 %copy-start.7 = (f32[512,1024]{1,0:T(8,128)S(1)}, f32[512,1024]{1,0:T(8,128)}, u32[]{:S(2)}) copy-start(f32[512,1024]{1,0:T(8,128)} %copy-done.6) | copy-start | bytes 6291460
  444.6 97.0 %all-gather.25.cloned.1.call-start = ((), (), s32[]{:S(2)}) async-start(), calls=%async_computation.6 | async-start | bytes 6291456 | tf_op jit(solution)/shard_map/all_gather | solution.py:97
  472.7 1.3 copy-start.9
  474.0 48.8 %collective-permute-start.3 = (f32[512,1024]{1,0:T(8,128)S(1)}, f32[512,1024]{1,0:T(8,128)}, u32[]{:S(2)}, u32[]{:S(2)}) collective-permute-start(f32[512,1024]{1,0:T(8,128)S(1)} %convolution_select_fusion.2), channel_id=1, source_target_pairs={{0,8},{2,10},{4,12},{6,14},{8,16},{10,18},{12,20},{14,22},{16,24},... | collective-permute-start | bytes 6291464 | tf_op jit(solution)/shard_map/ppermute | solution.py:16
  478.8 62.9 %copy-start.10 = (f32[512,1024]{1,0:T(8,128)S(1)}, f32[512,1024]{1,0:T(8,128)}, u32[]{:S(2)}) copy-start(f32[512,1024]{1,0:T(8,128)} %copy-done.9) | copy-start | bytes 6291460
  522.8 99.8 %all-gather.27.cloned.1.call-start = ((), (), s32[]{:S(2)}) async-start(), calls=%async_computation.7 | async-start | bytes 6291456 | tf_op jit(solution)/shard_map/all_gather | solution.py:97
  550.8 1.3 copy-start.12
  552.1 50.3 %collective-permute-start.4 = (f32[512,1024]{1,0:T(8,128)S(1)}, f32[512,1024]{1,0:T(8,128)S(1)}, u32[]{:S(2)}, u32[]{:S(2)}) collective-permute-start(f32[512,1024]{1,0:T(8,128)S(1)} %convolution_select_fusion.1), channel_id=1, source_target_pairs={{0,16},{2,18},{4,20},{6,22},{8,24},{10,26},{12,28},{14,30},{16,32}... | collective-permute-start | bytes 6291464 | tf_op jit(solution)/shard_map/ppermute | solution.py:16
  602.5 1.4 copy-start.14
  603.8 233.1 %all-gather.29.cloned.1.call-start = ((), (), s32[]{:S(2)}) async-start(), calls=%async_computation.8 | async-start | bytes 6291456 | tf_op jit(solution)/shard_map/all_gather | solution.py:97
  632.7 48.9 %copy-start.16 = (bf16[2048]{0:T(1024)(128)(2,1)S(1)}, bf16[2048]{0:T(1024)(128)(2,1)}, u32[]{:S(2)}) copy-start(bf16[2048]{0:T(1024)(128)(2,1)} %param.8) | copy-start | bytes 12292
  632.7 48.9 %collective-permute-start.5 = (f32[512,1024]{1,0:T(8,128)S(1)}, f32[512,1024]{1,0:T(8,128)}, u32[]{:S(2)}, u32[]{:S(2)}) collective-permute-start(f32[512,1024]{1,0:T(8,128)S(1)} %convolution_select_fusion), channel_id=1, source_target_pairs={{0,32},{2,34},{4,36},{6,38},{8,40},{10,42},{12,44},{14,46},{16,48}... | collective-permute-start | bytes 6291464 | tf_op jit(solution)/shard_map/ppermute | solution.py:16
  753.3 6.7 copy-start.1
  758.0 7.6 copy-start.17
  758.0 14.9 %copy-start.5 = (f32[512,1024]{1,0:T(8,128)S(1)}, f32[512,1024]{1,0:T(8,128)}, u32[]{:S(2)}) copy-start(f32[512,1024]{1,0:T(8,128)} %copy-done.4) | copy-start | bytes 6291460
  759.9 22.7 %copy-start.8 = (f32[512,1024]{1,0:T(8,128)S(1)}, f32[512,1024]{1,0:T(8,128)}, u32[]{:S(2)}) copy-start(f32[512,1024]{1,0:T(8,128)} %copy-done.6) | copy-start | bytes 6291460
  761.8 3.8 collective-permute-start.6
  765.7 5.5 collective-permute-start.7
  772.9 24.9 %copy-start.11 = (f32[512,1024]{1,0:T(8,128)S(1)}, f32[512,1024]{1,0:T(8,128)}, u32[]{:S(2)}) copy-start(f32[512,1024]{1,0:T(8,128)} %copy-done.9) | copy-start | bytes 6291460
  774.8 6.0 collective-permute-start.8
  782.6 25.0 %copy-start.13 = (f32[512,1024]{1,0:T(8,128)S(1)}, f32[512,1024]{1,0:T(8,128)}, u32[]{:S(2)}) copy-start(f32[512,1024]{1,0:T(8,128)} %copy-done.12) | copy-start | bytes 6291460
  784.5 11.6 %collective-permute-start.9 = (f32[512]{0:T(512)S(1)}, f32[512]{0:T(512)S(1)}, u32[]{:S(2)}, u32[]{:S(2)}) collective-permute-start(f32[512]{0:T(512)S(1)} %add_select_fusion.4), channel_id=1, source_target_pairs={{0,8},{2,10},{4,12},{6,14},{8,16},{10,18},{12,20},{14,22},{16,24},... | collective-permute-start | bytes 6152 | tf_op jit(solution)/shard_map/ppermute | solution.py:16
  799.7 6.1 collective-permute-start.10
  809.4 15.7 %collective-permute-start.11 = (f32[512]{0:T(512)S(1)}, f32[512]{0:T(512)S(1)}, u32[]{:S(2)}, u32[]{:S(2)}) collective-permute-start(f32[512]{0:T(512)S(1)} %add_select_fusion.2), channel_id=1, source_target_pairs={{0,32},{2,34},{4,36},{6,38},{8,40},{10,42},{12,44},{14,46},{16,48}... | collective-permute-start | bytes 6152 | tf_op jit(solution)/shard_map/ppermute | solution.py:16
  828.8 6.1 collective-permute-start.12
  846.1 3.9 copy-start.3
  848.0 5.6 copy-start.2
Sparse Core Ops, SparseCore 0:
  178.6 29.8 all-gather.16
  235.5 17.6 all-gather.18
  362.8 22.2 all-gather.20
  444.8 18.7 all-gather.22
  522.9 18.6 all-gather.24
  604.0 18.5 all-gather.26
  681.7 18.6 all-gather.28
where the time goes:
time: 869 us; the launch traced here: 863 us
  waiting for transfers between devices  384 us (44%)
  blocking collectives  147 us (17%)
  local copies, waits for them, and re-layouts  116 us (13%)
  matrix products  115 us (13%)
  starting transfers between devices  80.3 us (9%)
  between operations  14.2 us (2%)
    ppermute x13, waiting for transfers between devices, shifted(): lax.ppermute(value, axis, [(source, source + steps) for source in range(f...  274 us
    all_to_all x1, blocking collectives, body(): lax.all_to_all(send_rows, 'tm', split_axis=1, concat_axis=1, tiled=True)  110 us
    ppermute x13, starting transfers between devices, shifted(): lax.ppermute(value, axis, [(source, source + steps) for source in range(f...  79.1 us
    all_gather x5, waiting for transfers between devices, body(): lax.all_gather(recv_matrix, 'row', axis=0, tiled=True)  78.6 us
    dot_general x6, matrix products, left_product(): new_matrix = jnp.dot(left_rows, pieces[0], precision=lax.Precision.HIGHEST)  56.1 us
    gather x1, local copies, waits for them, and re-layouts, body(): padded_values[slot_table].reshape(SLAB_DEV, time_devs, capacity)  50.7 us
    gather x1, local copies, waits for them, and re-layouts, body(): padded_rows[slot_table].reshape(SLAB_DEV, time_devs, capacity, local_cols)  33.8 us
    all_gather x1, waiting for transfers between devices, body(): lax.all_gather(slab_rows, 'row', axis=2, tiled=True)  24.8 us
  transfers between devices with their start and end apart: 20, of which 19 were waited for; matrix products, arithmetic and copies ran while one was open for 9% of the time, Pallas kernels for 0%

commit v1 on v0

v1 whole, which is shorter than its diff:
```python
import jax
import jax.numpy as jnp
from jax import lax
from jax.experimental import pallas as pl
from jax.experimental.pallas import tpu as pltpu
from jax.sharding import PartitionSpec as P

F32 = jnp.float32
BF16 = jnp.bfloat16
I32 = jnp.int32
OBS = 2048
CAP = 64
COLS = 512
STATE = 1024
SLABS = 128
TIME_DEVS = 64
BLOCK_SLABS = 8
INFO_ROWS = 1024
GAIN = 0.3


def owner_of(position):
    return position ^ (((position >> 4) & 1) * 12)


def dispatch_kernel(target_ref, value_ref, rows_ref, send_ref, moment_ref, slot_ref):
    step = pl.program_id(0)

    @pl.when(step == 0)
    def _():
        chunk = 256
        row = lax.broadcasted_iota(I32, (chunk, chunk), 0)
        col = lax.broadcasted_iota(I32, (chunk, chunk), 1)
        before = (row < col).astype(F32).astype(BF16)
        carry = jnp.zeros((SLABS, 1), F32)
        moment = jnp.zeros((SLABS, COLS), F32)
        for index in range(OBS // chunk):
            part = pl.ds(index * chunk, chunk)
            target = target_ref[:, part]
            member = (lax.broadcasted_iota(I32, (SLABS, chunk), 0) == target).astype(F32)
            earlier = jnp.dot(member.astype(BF16), before, preferred_element_type=F32) + carry
            rank = jnp.sum(member * earlier, axis=0, keepdims=True).astype(I32)
            carry = carry + jnp.sum(member, axis=1, keepdims=True)
            owner = (target & 1) * TIME_DEVS + owner_of(target >> 1)
            slot_ref[:, part] = owner * CAP + rank
            weighted = (member * value_ref[:, part]).astype(BF16)
            moment = moment + jnp.dot(weighted, rows_ref[part, :], preferred_element_type=F32)
        moment_ref[...] = moment

    slots = BLOCK_SLABS * CAP
    here = lax.broadcasted_iota(I32, (slots, OBS), 0) + step * slots
    pick = jnp.where(here == slot_ref[...], 1.0, 0.0).astype(BF16)
    sent = jnp.dot(pick, rows_ref[...], preferred_element_type=F32).astype(BF16)
    send_ref[...] = sent.reshape(BLOCK_SLABS, CAP, COLS)


def dispatch(target, value, rows):
    whole = lambda i: (0, 0)
    return pl.pallas_call(
        dispatch_kernel,
        grid=(SLABS // BLOCK_SLABS,),
        in_specs=[
            pl.BlockSpec((1, OBS), whole),
            pl.BlockSpec((1, OBS), whole),
            pl.BlockSpec((OBS, COLS), whole),
        ],
        out_specs=[
            pl.BlockSpec((BLOCK_SLABS, CAP, COLS), lambda i: (i, 0, 0)),
            pl.BlockSpec((SLABS, COLS), whole),
        ],
        out_shape=[
            jax.ShapeDtypeStruct((SLABS, CAP, COLS), BF16),
            jax.ShapeDtypeStruct((SLABS, COLS), F32),
        ],
        scratch_shapes=[pltpu.VMEM((1, OBS), I32)],
        compiler_params=pltpu.CompilerParams(vmem_limit_bytes=48 * 2**20),
    )(target, value, rows)


def info_kernel(rows_ref, info_ref):
    step = pl.program_id(0)

    @pl.when(step == 0)
    def _():
        info_ref[...] = jnp.zeros_like(info_ref)

    left, right = rows_ref[0], rows_ref[1]

    def gram(a, b):
        return lax.dot_general(a, b, (((0,), (0,)), ((), ())), preferred_element_type=F32)

    info_ref[:COLS, :COLS] += gram(left, left)
    info_ref[:COLS, COLS:] += gram(left, right)
    info_ref[COLS:, COLS:] += gram(right, right)

    @pl.when(step == pl.num_programs(0) - 1)
    def _():
        info_ref[COLS:, :COLS] = info_ref[:COLS, COLS:].T


def information(halves):
    count = halves.shape[1]
    return pl.pallas_call(
        info_kernel,
        grid=(count // INFO_ROWS,),
        in_specs=[pl.BlockSpec((2, INFO_ROWS, COLS), lambda i: (0, i, 0))],
        out_specs=pl.BlockSpec((STATE, STATE), lambda i: (0, 0)),
        out_shape=jax.ShapeDtypeStruct((STATE, STATE), F32),
        compiler_params=pltpu.CompilerParams(vmem_limit_bytes=48 * 2**20),
    )(halves)


def apply(matrix_t, vector):
    return jnp.sum(matrix_t * vector[:, None], axis=0)


def body(initial, dynamics, obs_rows, obs_values, obs_slab):
    row_index = lax.axis_index("row")
    position = owner_of(lax.axis_index("tm"))
    second = row_index == 1
    swap = [(0, 1), (1, 0)]
    send, partial = dispatch(
        obs_slab.reshape(1, OBS), obs_values.astype(F32).reshape(1, OBS), obs_rows
    )
    moments = lax.psum(partial, "tm")
    received = lax.all_to_all(send, ("row", "tm"), split_axis=0, concat_axis=0, tiled=True)
    info = information(received.reshape(2, TIME_DEVS * CAP, COLS))
    evolve_t = jnp.eye(STATE, dtype=F32) + dynamics.T
    own_t = evolve_t - GAIN * jnp.dot(evolve_t, info, precision=lax.Precision.HIGH)
    other_t = lax.ppermute(own_t, "row", swap)
    first_t = jnp.where(second, other_t, own_t)
    last_t = jnp.where(second, own_t, other_t)
    both_t = jnp.dot(first_t, last_t, precision=lax.Precision.HIGH)

    mine = GAIN * lax.dynamic_slice(moments, (2 * position, 0), (2, COLS))
    theirs = lax.ppermute(mine, "row", swap)
    offsets = jnp.where(
        second,
        jnp.concatenate([theirs, mine], axis=1),
        jnp.concatenate([mine, theirs], axis=1),
    )
    offset = apply(last_t, offsets[0]) + offsets[1]

    ring = [(owner_of(t), owner_of((t + 1) % TIME_DEVS)) for t in range(TIME_DEVS)]
    at_start = position == 0
    after = jnp.zeros_like(initial)
    for step in range(TIME_DEVS):
        arrived = lax.ppermute(after, "tm", ring) if step else after
        before = jnp.where(at_start, initial, arrived)
        after = apply(both_t, before) + offset
    middle = apply(first_t, before) + offsets[0]
    states = jnp.stack([middle, after])
    states = jnp.where(second, states[:, COLS:], states[:, :COLS])
    home = [(owner_of(t), t) for t in range(TIME_DEVS)]
    return lax.ppermute(states, "tm", home)


def solution(mesh):
    placed = (P(), P(), P("tm", "row"), P("tm"), P("tm", None))
    return jax.shard_map(
        body, mesh=mesh, in_specs=placed, out_specs=P("tm", "row"), check_vma=False
    )
```

time: 869 us -> 799 us (0.919)
  waiting for transfers between devices: 384 us -> 670 us
  blocking collectives: 147 us -> 0 us
  local copies, waits for them, and re-layouts: 116 us -> 8.26 us
  matrix products: 115 us -> 19.4 us
  starting transfers between devices: 80.3 us -> 19.2 us
  Pallas kernels: 0 us -> 31.3 us
  other arithmetic: 7.01 us -> 29.2 us
    ppermute x13 -> x66, waiting for transfers between devices: 274 us -> 436 us  [the longest x63 435 us: body(): arrived = lax.ppermute(after, 'tm', ring) if step else after]
    all_to_all x2 -> x0, blocking collectives: 131 us -> none  [the longest x1 110 us: body(): lax.all_to_all(send_rows, 'tm', split_axis=1, concat_axis=1, tiled=True)]
    psum x0 -> x1, waiting for transfers between devices: none -> 125 us  [body(): moments = lax.psum(partial, 'tm')]
    all_gather x7 -> x0, waiting for transfers between devices: 110 us -> none  [the longest x5 78.6 us: body(): lax.all_gather(recv_matrix, 'row', axis=0, tiled=True)]
    all_to_all x0 -> x1, waiting for transfers between devices: none -> 109 us  [body(): lax.all_to_all(send, ('row', 'tm'), split_axis=0, concat_axis=0, tiled=True)]
    dot_general x19 -> x2, matrix products: 115 us -> 19.4 us  [the longest x1 10.7 us: body(): both_t = jnp.dot(first_t, last_t, precision=lax.Precision.HIGH)]
    gather x2 -> x0, local copies, waits for them, and re-layouts: 84.5 us -> none  [the longest x1 50.7 us: body(): padded_values[slot_table].reshape(SLAB_DEV, time_devs, capacity)]
    ppermute x13 -> x66, starting transfers between devices: 79.1 us -> 7.49 us  [the longest x63 6.38 us: body(): arrived = lax.ppermute(after, 'tm', ring) if step else after]
  transfers between devices with their start and end apart: 20 -> 68, of which waited for: 19 -> 66; matrix products, arithmetic and copies ran while one was open for 9% -> 1% of each run, Pallas kernels for 0% -> 0%
where the time goes in v1:
time: 799 us; the launch traced here: 792 us
  waiting for transfers between devices  670 us (84%)
  Pallas kernels  31.3 us (4%)
  other arithmetic  29.2 us (4%)
  matrix products  19.4 us (2%)
  starting transfers between devices  19.2 us (2%)
  between operations  15.1 us (2%)
  local copies, waits for them, and re-layouts  8.26 us (1%)
    ppermute x63, waiting for transfers between devices, body(): arrived = lax.ppermute(after, 'tm', ring) if step else after  435 us
    psum x1, waiting for transfers between devices, body(): moments = lax.psum(partial, 'tm')  125 us
    all_to_all x1, waiting for transfers between devices, body(): lax.all_to_all(send, ('row', 'tm'), split_axis=0, concat_axis=0, tiled=True)  109 us
    reduce_sum x64, other arithmetic, apply(): return jnp.sum(matrix_t * vector[:, None], axis=0)  27.2 us
    pallas_call x1, Pallas kernels, dispatch(): pl.pallas_call(dispatch_kernel, grid=(SLABS // BLOCK_SLABS,), in_specs=[p...  21.6 us
  transfers between devices with their start and end apart: 68, of which 66 were waited for; matrix products, arithmetic and copies ran while one was open for 1% of the time, Pallas kernels for 0%

profile of v1, /device:TPU:0, one launch (start us, length us, event | category | flops | bytes accessed | tf_op | source)
XLA Modules:
  0.0 792.2 jit_solution(6095948547946350420)
XLA Ops:
  9.5 21.6 %shard_map.55 = (bf16[128,64,512]{2,1,0:T(8,128)(2,1)}, f32[128,512]{1,0:T(8,128)}) custom-call(s32[1,2048]{1,0:T(1,128)S(1)} %bitcast.17, f32[1,2048]{1,0:T(1,128)S(1)} %bitcast.16, bf16[2048,512]{1,0:T(8,128)(2,1)S(1)} %copy-done), custom_call_target="tpu_custom_call" | custom-call | tf_op jit(solution)/shard_map/pallas_call | solution.py:59
  31.1 11.7 %all-to-all-start = ((bf16[128,64,512]{2,1,0:T(8,128)(2,1)}), bf16[128,64,512]{2,1,0:T(8,128)(2,1)}, u32[]{:S(2)}, u32[]{:S(2)}) async-start(bf16[128,64,512]{2,1,0:T(8,128)(2,1)} %get-tuple-element.7), calls=%async_computation | async-start | bytes 16777216 | tf_op jit(solution)/shard_map/all_to_all | solution.py:126
  48.2 108.6 %all-to-all-done = bf16[128,64,512]{2,1,0:T(8,128)(2,1)} async-done(((bf16[128,64,512]{2,1,0:T(8,128)(2,1)}), bf16[128,64,512]{2,1,0:T(8,128)(2,1)}, u32[]{:S(2)}, u32[]{:S(2)}) %all-to-all-start) | async-done | bytes 8388640 | tf_op jit(solution)/shard_map/all_to_all | solution.py:126
  156.8 9.7 %shard_map.56 = f32[1024,1024]{1,0:T(8,128)S(1)} custom-call(bf16[2,4096,512]{2,1,0:T(8,128)(2,1)} %bitcast.3.rows_ref), custom_call_target="tpu_custom_call" | custom-call | tf_op jit(solution)/shard_map/pallas_call | solution.py:103
  166.5 8.7 %multiply_subtract_fusion = f32[1024,1024]{1,0:T(8,128)} fusion(f32[1024,1024]{0,1:T(8,128)S(1)} %copy-done.3, f32[1024,1024]{1,0:T(8,128)S(1)} %shard_map.56), kind=kOutput, calls=%fused_computation.67 | convolution fusion | flops 6450839552 | bytes 12582912 | tf_op jit(solution)/shard_map/dot_general | solution.py:129
  175.2 125.3 %all-reduce.2.cloned.1.call-done = f32[128,512]{1,0:T(8,128)} async-done(((f32[128,512]{1,0:T(8,128)}), f32[128,512]{1,0:T(8,128)}) %all-reduce.2.cloned.1.call-update) | async-done | bytes 262160 | tf_op jit(solution)/shard_map/psum | solution.py:125
  302.9 10.7 %multiply_reduce_fusion.65 = (f32[1024]{0:T(1024)S(1)}, f32[1024,1024]{1,0:T(8,128)S(1)}) fusion(f32[1024]{0:T(1024)S(1)} %broadcast_select_fusion.4, f32[1024,1024]{1,0:T(8,128)} %multiply_subtract_fusion, f32[1024,1024]{1,0:T(8,128)} %collective-permute-done, pred[]{:T(512)S(6)} %eq.9), kind=kOutput, calls=%fused_computation.66 | convolution fusion | flops 6446644224 | bytes 12591105 | tf_op jit(solution)/shard_map/dot_general | solution.py:133
  323.8 6.9 collective-permute-done.3
  331.2 6.9 collective-permute-done.4
  338.5 6.9 collective-permute-done.5
  345.9 6.9 collective-permute-done.6
  353.3 6.9 collective-permute-done.7
  360.6 6.9 collective-permute-done.8
  368.0 6.9 collective-permute-done.9
  375.4 6.9 collective-permute-done.10
  382.7 6.9 collective-permute-done.11
  390.3 6.9 collective-permute-done.12
  397.6 6.9 collective-permute-done.13
  405.0 6.9 collective-permute-done.14
  412.4 6.9 collective-permute-done.15
  419.8 6.9 collective-permute-done.16
  427.1 6.9 collective-permute-done.17
  434.5 6.9 collective-permute-done.18
  441.9 6.9 collective-permute-done.19
  449.2 6.9 collective-permute-done.20
  456.6 6.9 collective-permute-done.21
  464.0 6.9 collective-permute-done.22
  471.3 6.9 collective-permute-done.23
  478.7 6.9 collective-permute-done.24
  486.1 6.9 collective-permute-done.25
  493.4 6.9 collective-permute-done.26
  500.8 6.9 collective-permute-done.27
  508.2 6.9 collective-permute-done.28
  515.9 6.9 collective-permute-done.29
  523.3 6.9 collective-permute-done.30
  530.7 6.9 collective-permute-done.31
  538.1 6.9 collective-permute-done.32
  545.4 6.9 collective-permute-done.33
  552.8 6.9 collective-permute-done.34
  560.2 6.9 collective-permute-done.35
  567.5 6.9 collective-permute-done.36
  574.9 6.9 collective-permute-done.37
  582.3 6.9 collective-permute-done.38
  589.6 6.9 collective-permute-done.39
  597.0 6.9 collective-permute-done.40
  604.4 6.9 collective-permute-done.41
  611.7 6.9 collective-permute-done.42
  619.1 6.9 collective-permute-done.43
  626.5 6.9 collective-permute-done.44
  633.8 6.9 collective-permute-done.45
  641.4 6.9 collective-permute-done.46
  648.8 6.9 collective-permute-done.47
  656.1 6.9 collective-permute-done.48
  663.5 6.9 collective-permute-done.49
  670.9 6.9 collective-permute-done.50
  678.2 6.9 collective-permute-done.51
  685.6 6.9 collective-permute-done.52
  693.0 6.9 collective-permute-done.53
  700.3 6.9 collective-permute-done.54
  707.7 6.9 collective-permute-done.55
  715.1 6.9 collective-permute-done.56
  722.4 6.9 collective-permute-done.57
  729.8 6.9 collective-permute-done.58
  774.0 6.9 collective-permute-done.64
  (284 shorter events, 86.7 us)
Async XLA Ops:
  31.1 125.6 %all-to-all-start = ((bf16[128,64,512]{2,1,0:T(8,128)(2,1)}), bf16[128,64,512]{2,1,0:T(8,128)(2,1)}, u32[]{:S(2)}, u32[]{:S(2)}) async-start(bf16[128,64,512]{2,1,0:T(8,128)(2,1)} %get-tuple-element.7), calls=%async_computation | async-start | bytes 16777216 | tf_op jit(solution)/shard_map/all_to_all | solution.py:126
  42.8 257.8 %all-reduce.2.cloned.1.call-start = ((), (), s32[]{:S(2)}) async-start(), calls=%async_computation.1 | async-start | bytes 524288 | tf_op jit(solution)/shard_map/psum | solution.py:125
  175.2 127.7 %collective-permute-start = (f32[1024,1024]{1,0:T(8,128)}, f32[1024,1024]{1,0:T(8,128)}, u32[]{:S(2)}, u32[]{:S(2)}) collective-permute-start(f32[1024,1024]{1,0:T(8,128)} %multiply_subtract_fusion), channel_id=1, source_target_pairs={{0,1},{1,0},{2,3},{3,2},{4,5},{5,4},{6,7},{7,6},{8,9},{9,8},{10,11... | collective-permute-start | bytes 12582920 | tf_op jit(solution)/shard_map/ppermute | solution.py:130
  316.3 7.0 collective-permute-start.2
  323.7 7.0 collective-permute-start.3
  331.1 7.0 collective-permute-start.4
  338.4 7.0 collective-permute-start.5
  345.8 7.0 collective-permute-start.6
  353.2 7.0 collective-permute-start.7
  360.5 7.0 collective-permute-start.8
  367.9 7.0 collective-permute-start.9
  375.3 7.0 collective-permute-start.10
  382.7 7.0 collective-permute-start.11
  390.0 7.2 collective-permute-start.12
  397.6 7.0 collective-permute-start.13
  404.9 7.0 collective-permute-start.14
  412.3 7.0 collective-permute-start.15
  419.7 7.0 collective-permute-start.16
  427.0 7.0 collective-permute-start.17
  434.4 7.0 collective-permute-start.18
  441.8 7.0 collective-permute-start.19
  449.1 7.0 collective-permute-start.20
  456.5 7.0 collective-permute-start.21
  463.9 7.0 collective-permute-start.22
  471.3 7.0 collective-permute-start.23
  478.6 7.0 collective-permute-start.24
  486.0 7.0 collective-permute-start.25
  493.4 7.0 collective-permute-start.26
  500.7 7.0 collective-permute-start.27
  508.1 7.0 collective-permute-start.28
  515.5 7.4 collective-permute-start.29
  523.2 7.0 collective-permute-start.30
  530.6 7.0 collective-permute-start.31
  538.0 7.0 collective-permute-start.32
  545.3 7.0 collective-permute-start.33
  552.7 7.0 collective-permute-start.34
  560.1 7.0 collective-permute-start.35
  567.4 7.0 collective-permute-start.36
  574.8 7.0 collective-permute-start.37
  582.2 7.0 collective-permute-start.38
  589.6 7.0 collective-permute-start.39
  596.9 7.0 collective-permute-start.40
  604.3 7.0 collective-permute-start.41
  611.7 7.0 collective-permute-start.42
  619.0 7.0 collective-permute-start.43
  626.4 7.0 collective-permute-start.44
  633.8 7.0 collective-permute-start.45
  641.1 7.2 collective-permute-start.46
  663.4 7.0 collective-permute-start.49
  670.8 7.0 collective-permute-start.50
  678.1 7.0 collective-permute-start.51
  685.5 7.0 collective-permute-start.52
  692.9 7.0 collective-permute-start.53
  700.2 7.0 collective-permute-start.54
  707.6 7.0 collective-permute-start.55
  715.0 7.0 collective-permute-start.56
  722.4 7.0 collective-permute-start.57
  729.7 7.0 collective-permute-start.58
  737.1 7.0 collective-permute-start.59
  744.5 7.0 collective-permute-start.60
  751.8 7.0 collective-permute-start.61
  759.2 7.0 collective-permute-start.62
  766.6 7.0 collective-permute-start.63
  773.9 7.0 collective-permute-start.64
  (8 other events, 163.5 us)
Sparse Core Ops, SparseCore 0:
  175.3 125.1 all-reduce.1
